TPU v7x, 1024 devices: a whole 8x8x8 slice. The times are simulated.
1024 devices in a mesh: dp: 64 (over z, x), tensor: 16 (over y, core).
Axes of the slice: x: 8, y: 8, z: 8, core: 2. Of those that a mesh axis runs over, the one named last changes fastest.
Arguments:
- grads: bfloat16 [64, 1024, 8192], P('dp', None, 'tensor'), may hold values from -60 to 60
- errors: bfloat16 [64, 1024, 8192], P('dp', None, 'tensor'), may hold values from -3 to 3
- q_in: float32 [1024, 4], replicated, may hold values from -6 to 6
Outputs:
- new_error: bfloat16 [64, 1024, 8192], P('dp', None, 'tensor')
- right_factor: float32 [8192, 4], P('tensor')
- new_q: float32 [1024, 4], replicated
All inputs are finite; a program needn't handle non-finite values.
Results may differ from a plain program's by a relative error of at most 0.001.
Values sent between devices are 32-bit elements; how exact they have to be, the bound alone decides.
No kernel may reach another device: no remote copies, remote signals or barrier semaphores. Data moves between devices by JAX's collectives and lax.ppermute only.
A program may use at most 32 MiB of HBM per device.

v0:
```python
import functools
import math

import jax
import jax.numpy as jnp
from jax import lax
from jax.experimental import pallas as pl
from jax.experimental.pallas import tpu as pltpu
from jax.sharding import Mesh
from jax.sharding import PartitionSpec as P

COLS = 8192
RANK = 4
LANES = 128
LOADS = 2
CHUNKS = 4
SENDER, SOLVER = 1, 0
VMEM = pl.BlockSpec(memory_space=pltpu.VMEM)
HBM = pl.BlockSpec(memory_space=pltpu.HBM)


def pieces_of(value):
    high = value.astype(jnp.bfloat16).astype(jnp.float32)
    rest = value - high
    middle = rest.astype(jnp.bfloat16).astype(jnp.float32)
    low = (rest - middle).astype(jnp.bfloat16).astype(jnp.float32)
    return high, middle, low


def stacked(*rows):
    rows += (jnp.zeros_like(rows[0]),) * (-len(rows) % (16 // RANK))
    return jnp.concatenate(rows, axis=0).astype(jnp.bfloat16)


def unstacked_sum(products):
    return products[:RANK] + (products[RANK : 2 * RANK] + products[2 * RANK : 3 * RANK])


def to_blocks(ref, value):
    for block in range(value.shape[1] // LANES):
        ref[block * RANK : (block + 1) * RANK, :] = value[:, block * LANES : (block + 1) * LANES]


def from_blocks(value):
    blocks = [value[row : row + RANK] for row in range(0, value.shape[0], RANK)]
    return jnp.concatenate(blocks, axis=1)


def inverse_root(value):
    root = lax.rsqrt(value)
    return root * (1.5 - 0.5 * value * root * root)


def inverse_columns(gram):
    shape = (RANK, LANES)
    lower, inverse = {}, {}
    for i in range(RANK):
        for j in range(i + 1):
            rest = jnp.broadcast_to(gram[i : i + 1, j : j + 1], shape)
            for k in range(j):
                rest = rest - lower[i, k] * lower[j, k]
            if j < i:
                lower[i, j] = rest * inverse[j, j]
            else:
                inverse[i, i] = inverse_root(rest)
    for i in range(RANK):
        for j in range(i):
            total = lower[i, j] * inverse[j, j]
            for k in range(j + 1, i):
                total = total + lower[i, k] * inverse[k, j]
            inverse[i, j] = -total * inverse[i, i]
    row = lax.broadcasted_iota(jnp.int32, shape, 0)
    columns = []
    for j in range(RANK):
        column = jnp.zeros(shape, jnp.float32)
        for i in range(j, RANK):
            column = jnp.where(row == i, inverse[i, j], column)
        columns.append(column)
    return columns


def multiplied(columns, block):
    total = columns[0] * block[:1]
    for j in range(1, RANK):
        total = total + columns[j] * block[j : j + 1]
    return total


def left_kernel(q_hbm, grads_hbm, errors_hbm, left_ref, grads_ref, errors_ref, q_ref, q_sem, sems):
    rows, cols = grads_ref.shape
    step = rows // LOADS
    q_copy = pltpu.make_async_copy(q_hbm, q_ref, q_sem)
    q_copy.start()
    copies = []
    for chunk in range(LOADS):
        part = pl.ds(chunk * step, step)
        for which, (source, target) in enumerate(((grads_hbm, grads_ref), (errors_hbm, errors_ref))):
            copy = pltpu.make_async_copy(source.at[0, part, :], target.at[part, :], sems.at[chunk, which])
            copy.start()
            copies.append(copy)
    q_copy.wait()
    q = stacked(*pieces_of(q_ref[...]))
    total = jnp.zeros((q.shape[0], cols), jnp.float32)
    for chunk in range(LOADS):
        part = pl.ds(chunk * step, step)
        for which, source in enumerate((grads_ref, errors_ref)):
            copies[2 * chunk + which].wait()
            total += jnp.dot(
                q[:, chunk * step : (chunk + 1) * step], source[part, :], preferred_element_type=jnp.float32
            )
    to_blocks(left_ref, unstacked_sum(total))


def back_kernel(replicas, parts_ref, grads_ref, errors_ref, left_ref, terms_ref):
    left = from_blocks(jnp.sum(parts_ref[...], axis=0)) * (1.0 / replicas)
    left_ref[...] = left
    stack = stacked(*pieces_of(left))
    across = (((1,), (1,)), ((), ()))
    total = lax.dot_general(stack, grads_ref[...], across, preferred_element_type=jnp.float32)
    total += lax.dot_general(stack, errors_ref[...], across, preferred_element_type=jnp.float32)
    back = unstacked_sum(total)
    gram = lax.dot_general(
        left, left, across, precision=lax.Precision.HIGHEST, preferred_element_type=jnp.float32
    )
    used = back.shape[1] // LANES * RANK
    to_blocks(terms_ref, back)
    terms_ref[used:, :] = jnp.zeros((terms_ref.shape[0] - used, LANES), jnp.float32)
    terms_ref[used : used + RANK, :RANK] = gram


def sum_kernel(parts_ref, out_ref):
    used = parts_ref.shape[1]
    out_ref[:used, :] = jnp.sum(parts_ref[...], axis=0)
    out_ref[used:, :] = jnp.zeros((out_ref.shape[0] - used, LANES), jnp.float32)


def inverse_kernel(parts_ref, out_ref):
    used = out_ref.shape[0] - RANK * RANK
    out_ref[:used, :] = jnp.zeros((used, LANES), jnp.float32)
    columns = inverse_columns(jnp.sum(parts_ref[...], axis=0)[:RANK])
    for j, column in enumerate(columns):
        out_ref[used + j * RANK : used + (j + 1) * RANK, :] = column


def error_kernel(
    replicas, terms_ref, left_ref, grads_ref, errors_ref, out_hbm, right_hbm, q_hbm, out_ref, right_ref, q_ref, sems
):
    rows, cols = grads_ref.shape
    used = rows // LANES * RANK
    inverse = [terms_ref[SOLVER, used + j * RANK : used + (j + 1) * RANK, :] for j in range(RANK)]
    right = jnp.concatenate(
        [multiplied(inverse, left_ref[:, start : start + LANES]) for start in range(0, cols, LANES)], axis=1
    )
    new_q = jnp.concatenate(
        [multiplied(inverse, terms_ref[SENDER, start : start + RANK, :]) for start in range(0, used, RANK)], axis=1
    ) * (1.0 / replicas)
    right_ref[...] = right * math.sqrt(COLS)
    q_ref[...] = new_q
    copies = [
        pltpu.make_async_copy(right_ref, right_hbm, sems.at[CHUNKS]),
        pltpu.make_async_copy(q_ref, q_hbm, sems.at[CHUNKS + 1]),
    ]
    for copy in copies:
        copy.start()
    q1, q2, q3 = pieces_of(new_q)
    r1, r2, r3 = pieces_of(right)
    tall = stacked(q1, q1, q2, q2, q1, q3)
    wide = stacked(r1, r2, r1, r2, r3, r1)
    step = rows // CHUNKS
    for chunk in range(CHUNKS):
        part = pl.ds(chunk * step, step)
        approx = lax.dot_general(
            tall[:, chunk * step : (chunk + 1) * step],
            wide,
            (((0,), (0,)), ((), ())),
            preferred_element_type=jnp.float32,
        )
        merged = grads_ref[part, :].astype(jnp.float32) + errors_ref[part, :].astype(jnp.float32)
        out_ref[part, :] = (merged - approx).astype(jnp.bfloat16)
        copy = pltpu.make_async_copy(out_ref.at[part, :], out_hbm.at[0, part, :], sems.at[chunk])
        copy.start()
        copies.append(copy)
    for copy in copies:
        copy.wait()


def copies_for(value, axis):
    return jnp.broadcast_to(value[None], (lax.axis_size(axis),) + value.shape)


def exchange(value, axis):
    return lax.all_to_all(copies_for(value, axis), axis, 0, 0, tiled=True)


def on_device(grads, errors, q_in):
    replicas = lax.axis_size("z") * lax.axis_size("x")
    _, rows, cols = grads.shape
    f32, bf16 = jnp.float32, jnp.bfloat16
    left_rows, back_rows = RANK * cols // LANES, RANK * rows // LANES
    limit = pltpu.CompilerParams(vmem_limit_bytes=32 * 2**20)
    q_in, core = lax.optimization_barrier((q_in, lax.axis_index("core")))

    left, grads_near, errors_near = pl.pallas_call(
        left_kernel,
        out_shape=(
            pltpu.VMEM((left_rows, LANES), f32),
            pltpu.VMEM((rows, cols), bf16),
            pltpu.VMEM((rows, cols), bf16),
        ),
        in_specs=[HBM] * 3,
        out_specs=(VMEM, VMEM, VMEM),
        scratch_shapes=[pltpu.VMEM((RANK, rows), f32), pltpu.SemaphoreType.DMA, pltpu.SemaphoreType.DMA((LOADS, 2))],
        compiler_params=limit,
        name="left",
    )(*(pltpu.with_memory_space_constraint(x, pltpu.HBM) for x in (q_in.T, grads, errors)))

    left = jnp.sum(exchange(left, "x"), axis=0)
    left, terms = pl.pallas_call(
        functools.partial(back_kernel, replicas),
        out_shape=(
            pltpu.VMEM((RANK, cols), f32),
            pltpu.VMEM((back_rows + 8, LANES), f32),
        ),
        in_specs=[VMEM] * 3,
        out_specs=(VMEM, VMEM),
        compiler_params=limit,
        name="back",
    )(exchange(left, "z"), grads_near, errors_near)

    terms = jnp.sum(lax.all_gather(terms, "core"), axis=0)

    def place(kernel, parts, name):
        shape = pltpu.VMEM((back_rows + RANK * RANK, LANES), f32)
        return pl.pallas_call(
            kernel, out_shape=shape, in_specs=[VMEM], out_specs=VMEM, compiler_params=limit, name=name
        )(parts)

    def sum_back(terms):
        back = jnp.sum(exchange(terms[:back_rows], "y"), axis=0)
        back = jnp.sum(exchange(back, "x"), axis=0)
        return place(sum_kernel, exchange(back, "z"), "sum")

    def invert_gram(terms):
        return place(inverse_kernel, exchange(terms[back_rows:], "y"), "inverse")

    terms, core = lax.optimization_barrier((terms, core))
    terms = lax.cond(core == SENDER, sum_back, invert_gram, terms)
    terms = lax.all_gather(terms, "core")

    new_error, right_factor, new_q = pl.pallas_call(
        functools.partial(error_kernel, replicas),
        out_shape=(
            jax.ShapeDtypeStruct((1, rows, cols), bf16),
            jax.ShapeDtypeStruct((RANK, cols), f32),
            jax.ShapeDtypeStruct((RANK, rows), f32),
        ),
        in_specs=[VMEM] * 4,
        out_specs=(HBM, HBM, HBM),
        scratch_shapes=[
            pltpu.VMEM((rows, cols), bf16),
            pltpu.VMEM((RANK, cols), f32),
            pltpu.VMEM((RANK, rows), f32),
            pltpu.SemaphoreType.DMA((CHUNKS + 2,)),
        ],
        compiler_params=limit,
        name="error",
    )(terms, left, grads_near, errors_near)
    return new_error, right_factor.T, new_q.T


def solution(mesh):
    physical = Mesh(mesh.devices.reshape(8, 8, 8, 2), ("z", "x", "y", "core"))
    dp, tensor = ("z", "x"), ("y", "core")
    return jax.shard_map(
        on_device,
        mesh=physical,
        in_specs=(P(dp, None, tensor), P(dp, None, tensor), P()),
        out_specs=(P(dp, None, tensor), P(tensor, None), P()),
        check_vma=False,
    )
```

profile of v0, /device:TPU:1, one launch (start us, length us, event | category | flops | bytes accessed | tf_op | source)
XLA Modules:
  0.0 85.2 jit_solution(16490229543369474236)
XLA Ops:
  0.6 1.8 %left.1 = (f32[16,128]{1,0:T(8,128)S(1)}, bf16[1024,512]{1,0:T(8,128)(2,1)S(1)}, bf16[1024,512]{1,0:T(8,128)(2,1)S(1)}) custom-call(f32[4,1024]{1,0:T(4,128)} %bitcast.7, bf16[1,1024,512]{2,1,0:T(8,128)(2,1)} %grads_hbm.1, bf16[1,1024,512]{2,1,0:T(8,128)(2,1)} %errors_hbm.1), custom_call_target="tpu_custom_call" | custom-call | tf_op jit(solution)/shard_map/left/pallas_call | solution.py:203
  2.4 14.3 %all_to_all.30 = f32[8,16,128]{2,1,0:T(8,128)S(1)} all-to-all(f32[8,16,128]{2,1,0:T(8,128)S(1)} %broadcast_in_dim.16), channel_id=1, replica_groups=mesh['z'=8,'x'=8,'y'=8,'core'=2] {'x'}, dimensions={0} | all-to-all | bytes 131072 | tf_op jit(solution)/shard_map/all_to_all | solution.py:192
  16.8 23.4 %all_to_all.31.parts_ref = f32[8,16,128]{2,1,0:T(8,128)S(1)} all-to-all(f32[8,16,128]{2,1,0:T(8,128)S(1)} %broadcast_in_dim.17), channel_id=1, replica_groups=mesh['z'=8,'x'=8,'y'=8,'core'=2] {'z'}, dimensions={0} | all-to-all | bytes 131072 | tf_op jit(solution)/shard_map/all_to_all | solution.py:192
  40.2 0.7 back.1
  40.9 5.0 %all-gather = f32[80,128]{1,0:T(8,128)S(1)} all-gather(f32[40,128]{1,0:T(8,128)S(1)} %get-tuple-element.24), channel_id=2, replica_groups=mesh['z'=8,'x'=8,'y'=8,'core'=2] {'core'}, dimensions={0}, use_global_device_ids=true | all-gather | bytes 61440 | tf_op jit(solution)/shard_map/all_gather | solution.py:230
  45.9 36.1 %conditional.1 = (f32[48,128]{1,0:T(8,128)S(1)}) conditional(s32[]{:T(128)} %convert_element_type.3, f32[40,128]{1,0:T(8,128)S(1)} %reduce_sum.37, f32[40,128]{1,0:T(8,128)S(1)} %reduce_sum.37), branch_computations={%region_2.0_spmd, %region_3.0_spmd} | conditional | flops 57344 | bytes 1556496 | solution.py:247
  45.9 15.4 %all_to_all.27 = f32[8,32,128]{2,1,0:T(8,128)S(1)} all-to-all(f32[8,32,128]{2,1,0:T(8,128)S(1)} %broadcast_in_dim.1), channel_id=1, replica_groups=mesh['z'=8,'x'=8,'y'=8,'core'=2] {'y'}, dimensions={0} | all-to-all | bytes 262144 | tf_op jit(solution)/shard_map/cond/branch_1_fun/all_to_all | solution.py:192
  61.4 10.3 %all_to_all.28 = f32[8,32,128]{2,1,0:T(8,128)S(1)} all-to-all(f32[8,32,128]{2,1,0:T(8,128)S(1)} %broadcast_in_dim.2), channel_id=1, replica_groups=mesh['z'=8,'x'=8,'y'=8,'core'=2] {'x'}, dimensions={0} | all-to-all | bytes 262144 | tf_op jit(solution)/shard_map/cond/branch_1_fun/all_to_all | solution.py:192
  71.7 10.3 %all_to_all.29.parts_ref = f32[8,32,128]{2,1,0:T(8,128)S(1)} all-to-all(f32[8,32,128]{2,1,0:T(8,128)S(1)} %broadcast_in_dim.4), channel_id=1, replica_groups=mesh['z'=8,'x'=8,'y'=8,'core'=2] {'z'}, dimensions={0} | all-to-all | bytes 262144 | tf_op jit(solution)/shard_map/cond/branch_1_fun/all_to_all | solution.py:192
  82.0 1.8 %all-gather.1 = f32[96,128]{1,0:T(8,128)S(1)} all-gather(f32[48,128]{1,0:T(8,128)S(1)} %get-tuple-element.32), channel_id=3, replica_groups=mesh['z'=8,'x'=8,'y'=8,'core'=2] {'core'}, dimensions={0}, use_global_device_ids=true | all-gather | bytes 73728 | tf_op jit(solution)/shard_map/all_gather | solution.py:248
  83.9 1.3 %error.1 = (bf16[1,1024,512]{2,1,0:T(8,128)(2,1)}, f32[4,512]{1,0:T(4,128)}, f32[4,1024]{1,0:T(4,128)}) custom-call(f32[2,48,128]{2,1,0:T(8,128)S(1)} %bitcast.5, f32[4,512]{1,0:T(4,128)S(1)} %get-tuple-element.28.left_ref, bf16[1024,512]{1,0:T(8,128)(2,1)S(1)} %get-tuple-element.22.grads_ref, bf16[1024,512]{1,0:T(8,128)(2,1)S(1)} %get-tuple-element.23.errors_ref), custom_call_target="tpu_custom_call" | custom-call | tf_op jit(solution)/shard_map/error/pallas_call | solution.py:250
  (11 shorter events, 0.1 us)
where the time goes:
time: 85.5 us; the launch traced here: 85.2 us
  blocking collectives  80.7 us (94%)
  Pallas kernels  3.73 us (4%)
    all_to_all x5, blocking collectives, exchange(): return lax.all_to_all(copies_for(value, axis), axis, 0, 0, tiled=True)  73.8 us
    all_gather x1, blocking collectives, on_device(): terms = jnp.sum(lax.all_gather(terms, 'core'), axis=0)  5.03 us
    all_gather x1, blocking collectives, on_device(): terms = lax.all_gather(terms, 'core')  1.84 us
    pallas_call x1, Pallas kernels, on_device(): pl.pallas_call(left_kernel, out_shape=(pltpu.VMEM((left_rows, LANES), f32...  1.76 us

commit v1 on v0

--- a/solution.py
+++ b/solution.py
@@ -15,6 +15,7 @@
 LOADS = 2
 CHUNKS = 4
 SENDER, SOLVER = 1, 0
+FEWER = 8
 VMEM = pl.BlockSpec(memory_space=pltpu.VMEM)
 HBM = pl.BlockSpec(memory_space=pltpu.HBM)
 
@@ -128,32 +129,26 @@
     terms_ref[used : used + RANK, :RANK] = gram
 
 
-def sum_kernel(parts_ref, out_ref):
-    used = parts_ref.shape[1]
-    out_ref[:used, :] = jnp.sum(parts_ref[...], axis=0)
-    out_ref[used:, :] = jnp.zeros((out_ref.shape[0] - used, LANES), jnp.float32)
-
-
-def inverse_kernel(parts_ref, out_ref):
-    used = out_ref.shape[0] - RANK * RANK
-    out_ref[:used, :] = jnp.zeros((used, LANES), jnp.float32)
-    columns = inverse_columns(jnp.sum(parts_ref[...], axis=0)[:RANK])
+def inverse_kernel(replicas, parts_ref, out_ref):
+    terms = jnp.sum(parts_ref[...], axis=0)
+    out_ref[:FEWER, :] = terms[:FEWER]
+    columns = inverse_columns(terms[FEWER : FEWER + RANK] * (1.0 / replicas))
     for j, column in enumerate(columns):
-        out_ref[used + j * RANK : used + (j + 1) * RANK, :] = column
+        out_ref[FEWER + j * RANK : FEWER + (j + 1) * RANK, :] = column
 
 
 def error_kernel(
     replicas, terms_ref, left_ref, grads_ref, errors_ref, out_hbm, right_hbm, q_hbm, out_ref, right_ref, q_ref, sems
 ):
     rows, cols = grads_ref.shape
-    used = rows // LANES * RANK
-    inverse = [terms_ref[SOLVER, used + j * RANK : used + (j + 1) * RANK, :] for j in range(RANK)]
+    inverse = [terms_ref[SOLVER, start : start + RANK, :] for start in range(FEWER, FEWER + RANK * RANK, RANK)]
+    more = rows // LANES * RANK - FEWER
+    blocks = [terms_ref[SENDER, start : start + RANK, :] for start in range(0, more, RANK)]
+    blocks += [terms_ref[SOLVER, start : start + RANK, :] for start in range(0, FEWER, RANK)]
     right = jnp.concatenate(
         [multiplied(inverse, left_ref[:, start : start + LANES]) for start in range(0, cols, LANES)], axis=1
     )
-    new_q = jnp.concatenate(
-        [multiplied(inverse, terms_ref[SENDER, start : start + RANK, :]) for start in range(0, used, RANK)], axis=1
-    ) * (1.0 / replicas)
+    new_q = jnp.concatenate([multiplied(inverse, block) for block in blocks], axis=1) * (1.0 / replicas)
     right_ref[...] = right * math.sqrt(COLS)
     q_ref[...] = new_q
     copies = [
@@ -184,12 +179,10 @@
         copy.wait()
 
 
-def copies_for(value, axis):
-    return jnp.broadcast_to(value[None], (lax.axis_size(axis),) + value.shape)
-
-
-def exchange(value, axis):
-    return lax.all_to_all(copies_for(value, axis), axis, 0, 0, tiled=True)
+def exchange(value, axes):
+    peers = math.prod(lax.axis_size(axis) for axis in axes)
+    copies = jnp.broadcast_to(value[None], (peers,) + value.shape)
+    return lax.all_to_all(copies, axes, 0, 0, tiled=True)
 
 
 def on_device(grads, errors, q_in):
@@ -214,7 +207,7 @@
         name="left",
     )(*(pltpu.with_memory_space_constraint(x, pltpu.HBM) for x in (q_in.T, grads, errors)))
 
-    left = jnp.sum(exchange(left, "x"), axis=0)
+    left = jnp.sum(exchange(left, ("x",)), axis=0)
     left, terms = pl.pallas_call(
         functools.partial(back_kernel, replicas),
         out_shape=(
@@ -225,26 +218,29 @@
         out_specs=(VMEM, VMEM),
         compiler_params=limit,
         name="back",
-    )(exchange(left, "z"), grads_near, errors_near)
+    )(exchange(left, ("z",)), grads_near, errors_near)
 
     terms = jnp.sum(lax.all_gather(terms, "core"), axis=0)
 
-    def place(kernel, parts, name):
-        shape = pltpu.VMEM((back_rows + RANK * RANK, LANES), f32)
+    near, far = ("x", "y_low"), ("z", "y_high")
+
+    def most(terms):
+        back = jnp.sum(exchange(terms[: back_rows - FEWER], near), axis=0)
+        return jnp.sum(exchange(back, far), axis=0)
+
+    def rest_and_inverse(terms):
+        terms = jnp.sum(exchange(terms[back_rows - FEWER :], far), axis=0)
         return pl.pallas_call(
-            kernel, out_shape=shape, in_specs=[VMEM], out_specs=VMEM, compiler_params=limit, name=name
-        )(parts)
-
-    def sum_back(terms):
-        back = jnp.sum(exchange(terms[:back_rows], "y"), axis=0)
-        back = jnp.sum(exchange(back, "x"), axis=0)
-        return place(sum_kernel, exchange(back, "z"), "sum")
-
-    def invert_gram(terms):
-        return place(inverse_kernel, exchange(terms[back_rows:], "y"), "inverse")
+            functools.partial(inverse_kernel, replicas),
+            out_shape=pltpu.VMEM((FEWER + RANK * RANK, LANES), f32),
+            in_specs=[VMEM],
+            out_specs=VMEM,
+            compiler_params=limit,
+            name="inverse",
+        )(exchange(terms, near))
 
     terms, core = lax.optimization_barrier((terms, core))
-    terms = lax.cond(core == SENDER, sum_back, invert_gram, terms)
+    terms = lax.cond(core == SENDER, most, rest_and_inverse, terms)
     terms = lax.all_gather(terms, "core")
 
     new_error, right_factor, new_q = pl.pallas_call(
@@ -269,8 +265,8 @@
 
 
 def solution(mesh):
-    physical = Mesh(mesh.devices.reshape(8, 8, 8, 2), ("z", "x", "y", "core"))
-    dp, tensor = ("z", "x"), ("y", "core")
+    physical = Mesh(mesh.devices.reshape(8, 8, 4, 2, 2), ("z", "x", "y_high", "y_low", "core"))
+    dp, tensor = ("z", "x"), ("y_high", "y_low", "core")
     return jax.shard_map(
         on_device,
         mesh=physical,

time: 85.5 us -> 82.7 us (0.967)
  blocking collectives: 80.7 us -> 77.8 us
    all_to_all x5 -> x4, blocking collectives: 73.8 us -> 71 us  [exchange(): return lax.all_to_all(copies, axes, 0, 0, tiled=True)]
where the time goes in v1:
time: 82.7 us; the launch traced here: 82.4 us
  blocking collectives  77.8 us (94%)
  Pallas kernels  3.71 us (4%)
    all_to_all x4, blocking collectives, exchange(): return lax.all_to_all(copies, axes, 0, 0, tiled=True)  71 us
    all_gather x1, blocking collectives, on_device(): terms = jnp.sum(lax.all_gather(terms, 'core'), axis=0)  5.03 us
    all_gather x1, blocking collectives, on_device(): terms = lax.all_gather(terms, 'core')  1.82 us
    pallas_call x1, Pallas kernels, on_device(): pl.pallas_call(left_kernel, out_shape=(pltpu.VMEM((left_rows, LANES), f32...  1.76 us

profile of v1, /device:TPU:1, one launch (start us, length us, event | category | flops | bytes accessed | tf_op | source)
XLA Modules:
  0.0 82.4 jit_solution(9929180361344885789)
XLA Ops:
  0.6 1.8 %left.1 = (f32[16,128]{1,0:T(8,128)S(1)}, bf16[1024,512]{1,0:T(8,128)(2,1)S(1)}, bf16[1024,512]{1,0:T(8,128)(2,1)S(1)}) custom-call(f32[4,1024]{1,0:T(4,128)} %bitcast.7, bf16[1,1024,512]{2,1,0:T(8,128)(2,1)} %grads_hbm.1, bf16[1,1024,512]{2,1,0:T(8,128)(2,1)} %errors_hbm.1), custom_call_target="tpu_custom_call" | custom-call | tf_op jit(solution)/shard_map/left/pallas_call | solution.py:196
  2.4 14.3 %all_to_all.30 = f32[8,16,128]{2,1,0:T(8,128)S(1)} all-to-all(f32[8,16,128]{2,1,0:T(8,128)S(1)} %broadcast_in_dim.12), channel_id=1, replica_groups=mesh['z'=8,'x'=8,'y_high'=4,'y_low'=2,'core'=2] {'x'}, dimensions={0} | all-to-all | bytes 131072 | tf_op jit(solution)/shard_map/all_to_all | solution.py:185
  16.8 23.4 %all_to_all.31.parts_ref = f32[8,16,128]{2,1,0:T(8,128)S(1)} all-to-all(f32[8,16,128]{2,1,0:T(8,128)S(1)} %broadcast_in_dim.13), channel_id=1, replica_groups=mesh['z'=8,'x'=8,'y_high'=4,'y_low'=2,'core'=2] {'z'}, dimensions={0} | all-to-all | bytes 131072 | tf_op jit(solution)/shard_map/all_to_all | solution.py:185
  40.2 0.7 back.1
  40.9 5.0 %all-gather = f32[80,128]{1,0:T(8,128)S(1)} all-gather(f32[40,128]{1,0:T(8,128)S(1)} %get-tuple-element.24), channel_id=2, replica_groups=mesh['z'=8,'x'=8,'y_high'=4,'y_low'=2,'core'=2] {'core'}, dimensions={0}, use_global_device_ids=true | all-gather | bytes 61440 | tf_op jit(solution)/shard_map/all_gather | solution.py:223
  45.9 33.3 %conditional.1 = (f32[24,128]{1,0:T(8,128)S(1)}) conditional(s32[]{:T(128)} %convert_element_type.3, f32[40,128]{1,0:T(8,128)S(1)} %reduce_sum.46, f32[40,128]{1,0:T(8,128)S(1)} %reduce_sum.46), branch_computations={%region_2.0_spmd, %region_4.0_spmd} | conditional | flops 141312 | bytes 2433040 | solution.py:243
  46.0 11.6 %all_to_all.28 = f32[16,24,128]{2,1,0:T(8,128)S(1)} all-to-all(f32[16,24,128]{2,1,0:T(8,128)S(1)} %broadcast_in_dim.2), channel_id=1, replica_groups=mesh['z'=8,'x'=8,'y_high'=4,'y_low'=2,'core'=2] {'x','y_low'}, dimensions={0} | all-to-all | bytes 393216 | tf_op jit(solution)/shard_map/cond/branch_1_fun/all_to_all | solution.py:185
  57.6 21.6 %all_to_all.29 = f32[32,24,128]{2,1,0:T(8,128)S(1)} all-to-all(f32[32,24,128]{2,1,0:T(8,128)S(1)} %broadcast_in_dim.3), channel_id=1, replica_groups=mesh['z'=8,'x'=8,'y_high'=4,'y_low'=2,'core'=2] {'z','y_high'}, dimensions={0} | all-to-all | bytes 786432 | tf_op jit(solution)/shard_map/cond/branch_1_fun/all_to_all | solution.py:185
  79.3 1.8 %all-gather.1 = f32[48,128]{1,0:T(8,128)S(1)} all-gather(f32[24,128]{1,0:T(8,128)S(1)} %get-tuple-element.32), channel_id=3, replica_groups=mesh['z'=8,'x'=8,'y_high'=4,'y_low'=2,'core'=2] {'core'}, dimensions={0}, use_global_device_ids=true | all-gather | bytes 36864 | tf_op jit(solution)/shard_map/all_gather | solution.py:244
  81.1 1.3 %error.1 = (bf16[1,1024,512]{2,1,0:T(8,128)(2,1)}, f32[4,512]{1,0:T(4,128)}, f32[4,1024]{1,0:T(4,128)}) custom-call(f32[2,24,128]{2,1,0:T(8,128)S(1)} %bitcast.5, f32[4,512]{1,0:T(4,128)S(1)} %get-tuple-element.28.left_ref, bf16[1024,512]{1,0:T(8,128)(2,1)S(1)} %get-tuple-element.22.grads_ref, bf16[1024,512]{1,0:T(8,128)(2,1)S(1)} %get-tuple-element.23.errors_ref), custom_call_target="tpu_custom_call" | custom-call | tf_op jit(solution)/shard_map/error/pallas_call | solution.py:246
  (9 shorter events, 0.1 us)

commit v2 on v1

--- a/solution.py
+++ b/solution.py
@@ -186,7 +186,7 @@
 
 
 def on_device(grads, errors, q_in):
-    replicas = lax.axis_size("z") * lax.axis_size("x")
+    replicas = math.prod(lax.axis_size(axis) for axis in ("z", "x_high", "x_low"))
     _, rows, cols = grads.shape
     f32, bf16 = jnp.float32, jnp.bfloat16
     left_rows, back_rows = RANK * cols // LANES, RANK * rows // LANES
@@ -207,7 +207,7 @@
         name="left",
     )(*(pltpu.with_memory_space_constraint(x, pltpu.HBM) for x in (q_in.T, grads, errors)))
 
-    left = jnp.sum(exchange(left, ("x",)), axis=0)
+    left = jnp.sum(exchange(left, ("x_high", "x_low")), axis=0)
     left, terms = pl.pallas_call(
         functools.partial(back_kernel, replicas),
         out_shape=(
@@ -222,7 +222,7 @@
 
     terms = jnp.sum(lax.all_gather(terms, "core"), axis=0)
 
-    near, far = ("x", "y_low"), ("z", "y_high")
+    near, far = ("y", "x_low"), ("z", "x_high")
 
     def most(terms):
         back = jnp.sum(exchange(terms[: back_rows - FEWER], near), axis=0)
@@ -265,8 +265,8 @@
 
 
 def solution(mesh):
-    physical = Mesh(mesh.devices.reshape(8, 8, 4, 2, 2), ("z", "x", "y_high", "y_low", "core"))
-    dp, tensor = ("z", "x"), ("y_high", "y_low", "core")
+    physical = Mesh(mesh.devices.reshape(8, 4, 2, 8, 2), ("z", "x_high", "x_low", "y", "core"))
+    dp, tensor = ("z", "x_high", "x_low"), ("y", "core")
     return jax.shard_map(
         on_device,
         mesh=physical,

time: 82.7 us -> 82.5 us (level)
    all_to_all x4, blocking collectives: 71 us -> 69.7 us  [exchange(): return lax.all_to_all(copies, axes, 0, 0, tiled=True)]
    all_gather x1, blocking collectives: 1.82 us -> 2.97 us  [on_device(): terms = lax.all_gather(terms, 'core')]
where the time goes in v2:
time: 82.5 us; the launch traced here: 82.2 us
  blocking collectives  77.7 us (94%)
  Pallas kernels  3.71 us (4%)
    all_to_all x4, blocking collectives, exchange(): return lax.all_to_all(copies, axes, 0, 0, tiled=True)  69.7 us
    all_gather x1, blocking collectives, on_device(): terms = jnp.sum(lax.all_gather(terms, 'core'), axis=0)  5.03 us
    all_gather x1, blocking collectives, on_device(): terms = lax.all_gather(terms, 'core')  2.97 us
    pallas_call x1, Pallas kernels, on_device(): pl.pallas_call(left_kernel, out_shape=(pltpu.VMEM((left_rows, LANES), f32...  1.76 us

profile of v2, /device:TPU:1, one launch (start us, length us, event | category | flops | bytes accessed | tf_op | source)
XLA Modules:
  0.0 82.2 jit_solution(10667215460681939845)
XLA Ops:
  0.6 1.8 %left.1 = (f32[16,128]{1,0:T(8,128)S(1)}, bf16[1024,512]{1,0:T(8,128)(2,1)S(1)}, bf16[1024,512]{1,0:T(8,128)(2,1)S(1)}) custom-call(f32[4,1024]{1,0:T(4,128)} %bitcast.7, bf16[1,1024,512]{2,1,0:T(8,128)(2,1)} %grads_hbm.1, bf16[1,1024,512]{2,1,0:T(8,128)(2,1)} %errors_hbm.1), custom_call_target="tpu_custom_call" | custom-call | tf_op jit(solution)/shard_map/left/pallas_call | solution.py:196
  2.4 14.3 %all_to_all.30 = f32[8,16,128]{2,1,0:T(8,128)S(1)} all-to-all(f32[8,16,128]{2,1,0:T(8,128)S(1)} %broadcast_in_dim.12), channel_id=1, replica_groups=mesh['z'=8,'x_high'=4,'x_low'=2,'y'=8,'core'=2] {'x_high','x_low'}, dimensions={0} | all-to-all | bytes 131072 | tf_op jit(solution)/shard_map/all_to_all | solution.py:185
  16.8 23.4 %all_to_all.31.parts_ref = f32[8,16,128]{2,1,0:T(8,128)S(1)} all-to-all(f32[8,16,128]{2,1,0:T(8,128)S(1)} %broadcast_in_dim.13), channel_id=1, replica_groups=mesh['z'=8,'x_high'=4,'x_low'=2,'y'=8,'core'=2] {'z'}, dimensions={0} | all-to-all | bytes 131072 | tf_op jit(solution)/shard_map/all_to_all | solution.py:185
  40.2 0.7 back.1
  40.9 5.0 %all-gather = f32[80,128]{1,0:T(8,128)S(1)} all-gather(f32[40,128]{1,0:T(8,128)S(1)} %get-tuple-element.24), channel_id=2, replica_groups=mesh['z'=8,'x_high'=4,'x_low'=2,'y'=8,'core'=2] {'core'}, dimensions={0}, use_global_device_ids=true | all-gather | bytes 61440 | tf_op jit(solution)/shard_map/all_gather | solution.py:223
  45.9 32.0 %conditional.1 = (f32[24,128]{1,0:T(8,128)S(1)}) conditional(s32[]{:T(128)} %convert_element_type.3, f32[40,128]{1,0:T(8,128)S(1)} %reduce_sum.46, f32[40,128]{1,0:T(8,128)S(1)} %reduce_sum.46), branch_computations={%region_2.0_spmd, %region_4.0_spmd} | conditional | flops 141312 | bytes 2433040 | solution.py:243
  46.0 15.8 %all_to_all.28 = f32[16,24,128]{2,1,0:T(8,128)S(1)} all-to-all(f32[16,24,128]{2,1,0:T(8,128)S(1)} %broadcast_in_dim.2), channel_id=1, replica_groups=mesh['z'=8,'x_high'=4,'x_low'=2,'y'=8,'core'=2] {'y','x_low'}, dimensions={0} | all-to-all | bytes 393216 | tf_op jit(solution)/shard_map/cond/branch_1_fun/all_to_all | solution.py:185
  61.8 16.1 %all_to_all.29 = f32[32,24,128]{2,1,0:T(8,128)S(1)} all-to-all(f32[32,24,128]{2,1,0:T(8,128)S(1)} %broadcast_in_dim.3), channel_id=1, replica_groups=mesh['z'=8,'x_high'=4,'x_low'=2,'y'=8,'core'=2] {'z','x_high'}, dimensions={0} | all-to-all | bytes 786432 | tf_op jit(solution)/shard_map/cond/branch_1_fun/all_to_all | solution.py:185
  77.9 3.0 %all-gather.1 = f32[48,128]{1,0:T(8,128)S(1)} all-gather(f32[24,128]{1,0:T(8,128)S(1)} %get-tuple-element.32), channel_id=3, replica_groups=mesh['z'=8,'x_high'=4,'x_low'=2,'y'=8,'core'=2] {'core'}, dimensions={0}, use_global_device_ids=true | all-gather | bytes 36864 | tf_op jit(solution)/shard_map/all_gather | solution.py:244
  80.9 1.3 %error.1 = (bf16[1,1024,512]{2,1,0:T(8,128)(2,1)}, f32[4,512]{1,0:T(4,128)}, f32[4,1024]{1,0:T(4,128)}) custom-call(f32[2,24,128]{2,1,0:T(8,128)S(1)} %bitcast.5, f32[4,512]{1,0:T(4,128)S(1)} %get-tuple-element.28.left_ref, bf16[1024,512]{1,0:T(8,128)(2,1)S(1)} %get-tuple-element.22.grads_ref, bf16[1024,512]{1,0:T(8,128)(2,1)S(1)} %get-tuple-element.23.errors_ref), custom_call_target="tpu_custom_call" | custom-call | tf_op jit(solution)/shard_map/error/pallas_call | solution.py:246
  (9 shorter events, 0.1 us)

commit v3 on v1

--- a/solution.py
+++ b/solution.py
@@ -112,8 +112,8 @@
     to_blocks(left_ref, unstacked_sum(total))
 
 
-def back_kernel(replicas, parts_ref, grads_ref, errors_ref, left_ref, terms_ref):
-    left = from_blocks(jnp.sum(parts_ref[...], axis=0)) * (1.0 / replicas)
+def back_kernel(replicas, sum_ref, grads_ref, errors_ref, left_ref, terms_ref):
+    left = from_blocks(sum_ref[...]) * (1.0 / replicas)
     left_ref[...] = left
     stack = stacked(*pieces_of(left))
     across = (((1,), (1,)), ((), ()))
@@ -207,7 +207,15 @@
         name="left",
     )(*(pltpu.with_memory_space_constraint(x, pltpu.HBM) for x in (q_in.T, grads, errors)))
 
-    left = jnp.sum(exchange(left, ("x",)), axis=0)
+    def in_two(left):
+        left = jnp.sum(exchange(left, ("x",)), axis=0)
+        return jnp.sum(exchange(left, ("z",)), axis=0)
+
+    def in_one(left):
+        return jnp.sum(exchange(left, ("z", "x")), axis=0)
+
+    left, core = lax.optimization_barrier((left, core))
+    left = lax.cond(core == SENDER, in_two, in_one, left)
     left, terms = pl.pallas_call(
         functools.partial(back_kernel, replicas),
         out_shape=(
@@ -218,7 +226,7 @@
         out_specs=(VMEM, VMEM),
         compiler_params=limit,
         name="back",
-    )(exchange(left, ("z",)), grads_near, errors_near)
+    )(left, grads_near, errors_near)
 
     terms = jnp.sum(lax.all_gather(terms, "core"), axis=0)
 

time: 82.7 us -> 82.4 us (level)
    all_gather x1, blocking collectives: 5.03 us -> 2.16 us  [on_device(): terms = jnp.sum(lax.all_gather(terms, 'core'), axis=0)]
    all_to_all x4, blocking collectives: 71 us -> 73.1 us  [exchange(): return lax.all_to_all(copies, axes, 0, 0, tiled=True)]
where the time goes in v3:
time: 82.4 us; the launch traced here: 82.1 us
  blocking collectives  77.6 us (94%)
  Pallas kernels  3.71 us (5%)
    all_to_all x4, blocking collectives, exchange(): return lax.all_to_all(copies, axes, 0, 0, tiled=True)  73.1 us
    all_gather x1, blocking collectives, on_device(): terms = lax.all_gather(terms, 'core')  2.32 us
    all_gather x1, blocking collectives, on_device(): terms = jnp.sum(lax.all_gather(terms, 'core'), axis=0)  2.16 us
    pallas_call x1, Pallas kernels, on_device(): pl.pallas_call(left_kernel, out_shape=(pltpu.VMEM((left_rows, LANES), f32...  1.76 us

profile of v3, /device:TPU:1, one launch (start us, length us, event | category | flops | bytes accessed | tf_op | source)
XLA Modules:
  0.0 82.1 jit_solution(11917268886098264818)
XLA Ops:
  0.6 1.8 %left.1 = (f32[16,128]{1,0:T(8,128)S(1)}, bf16[1024,512]{1,0:T(8,128)(2,1)S(1)}, bf16[1024,512]{1,0:T(8,128)(2,1)S(1)}) custom-call(f32[4,1024]{1,0:T(4,128)} %bitcast.7, bf16[1,1024,512]{2,1,0:T(8,128)(2,1)} %grads_hbm.1, bf16[1,1024,512]{2,1,0:T(8,128)(2,1)} %errors_hbm.1), custom_call_target="tpu_custom_call" | custom-call | tf_op jit(solution)/shard_map/left/pallas_call | solution.py:196
  2.4 38.9 %conditional.2 = (f32[16,128]{1,0:T(8,128)S(1)}) conditional(s32[]{:T(128)} %convert_element_type.6, f32[16,128]{1,0:T(8,128)S(1)} %get-tuple-element.31, f32[16,128]{1,0:T(8,128)S(1)} %get-tuple-element.31), branch_computations={%region_0.0_spmd, %region_2.0_spmd} | conditional | flops 129024 | bytes 2113548 | solution.py:218
  2.4 14.3 %all_to_all.29 = f32[8,16,128]{2,1,0:T(8,128)S(1)} all-to-all(f32[8,16,128]{2,1,0:T(8,128)S(1)} %broadcast_in_dim.10), channel_id=1, replica_groups=mesh['z'=8,'x'=8,'y_high'=4,'y_low'=2,'core'=2] {'x'}, dimensions={0} | all-to-all | bytes 131072 | tf_op jit(solution)/shard_map/cond/branch_1_fun/all_to_all | solution.py:185
  16.8 24.5 %all_to_all.30 = f32[8,16,128]{2,1,0:T(8,128)S(1)} all-to-all(f32[8,16,128]{2,1,0:T(8,128)S(1)} %broadcast_in_dim.11), channel_id=1, replica_groups=mesh['z'=8,'x'=8,'y_high'=4,'y_low'=2,'core'=2] {'z'}, dimensions={0} | all-to-all | bytes 131072 | tf_op jit(solution)/shard_map/cond/branch_1_fun/all_to_all | solution.py:185
  41.3 0.7 back.1
  42.0 2.2 %all-gather = f32[80,128]{1,0:T(8,128)S(1)} all-gather(f32[40,128]{1,0:T(8,128)S(1)} %get-tuple-element.34), channel_id=2, replica_groups=mesh['z'=8,'x'=8,'y_high'=4,'y_low'=2,'core'=2] {'core'}, dimensions={0}, use_global_device_ids=true | all-gather | bytes 61440 | tf_op jit(solution)/shard_map/all_gather | solution.py:231
  44.1 34.4 %conditional.3 = (f32[24,128]{1,0:T(8,128)S(1)}) conditional(s32[]{:T(128)} %convert_element_type.7, f32[40,128]{1,0:T(8,128)S(1)} %reduce_sum.63, f32[40,128]{1,0:T(8,128)S(1)} %reduce_sum.63), branch_computations={%region_6.0_spmd, %region_8.0_spmd} | conditional | flops 141312 | bytes 2433040 | solution.py:251
  44.1 13.9 %all_to_all.33 = f32[16,24,128]{2,1,0:T(8,128)S(1)} all-to-all(f32[16,24,128]{2,1,0:T(8,128)S(1)} %broadcast_in_dim.24), channel_id=1, replica_groups=mesh['z'=8,'x'=8,'y_high'=4,'y_low'=2,'core'=2] {'x','y_low'}, dimensions={0} | all-to-all | bytes 393216 | tf_op jit(solution)/shard_map/cond/branch_1_fun/all_to_all | solution.py:185
  58.1 20.4 %all_to_all.34 = f32[32,24,128]{2,1,0:T(8,128)S(1)} all-to-all(f32[32,24,128]{2,1,0:T(8,128)S(1)} %broadcast_in_dim.25), channel_id=1, replica_groups=mesh['z'=8,'x'=8,'y_high'=4,'y_low'=2,'core'=2] {'z','y_high'}, dimensions={0} | all-to-all | bytes 786432 | tf_op jit(solution)/shard_map/cond/branch_1_fun/all_to_all | solution.py:185
  78.6 2.3 %all-gather.1 = f32[48,128]{1,0:T(8,128)S(1)} all-gather(f32[24,128]{1,0:T(8,128)S(1)} %get-tuple-element.42), channel_id=3, replica_groups=mesh['z'=8,'x'=8,'y_high'=4,'y_low'=2,'core'=2] {'core'}, dimensions={0}, use_global_device_ids=true | all-gather | bytes 36864 | tf_op jit(solution)/shard_map/all_gather | solution.py:252
  80.9 1.3 %error.1 = (bf16[1,1024,512]{2,1,0:T(8,128)(2,1)}, f32[4,512]{1,0:T(4,128)}, f32[4,1024]{1,0:T(4,128)}) custom-call(f32[2,24,128]{2,1,0:T(8,128)S(1)} %bitcast.5, f32[4,512]{1,0:T(4,128)S(1)} %get-tuple-element.37.left_ref, bf16[1024,512]{1,0:T(8,128)(2,1)S(1)} %get-tuple-element.32.grads_ref, bf16[1024,512]{1,0:T(8,128)(2,1)S(1)} %get-tuple-element.33.errors_ref), custom_call_target="tpu_custom_call" | custom-call | tf_op jit(solution)/shard_map/error/pallas_call | solution.py:254
  (10 shorter events, 0.1 us)

commit v4 on v1

--- a/solution.py
+++ b/solution.py
@@ -15,7 +15,7 @@
 LOADS = 2
 CHUNKS = 4
 SENDER, SOLVER = 1, 0
-FEWER = 8
+FEWER = 2
 VMEM = pl.BlockSpec(memory_space=pltpu.VMEM)
 HBM = pl.BlockSpec(memory_space=pltpu.HBM)
 
@@ -123,28 +123,27 @@
     gram = lax.dot_general(
         left, left, across, precision=lax.Precision.HIGHEST, preferred_element_type=jnp.float32
     )
-    used = back.shape[1] // LANES * RANK
-    to_blocks(terms_ref, back)
-    terms_ref[used:, :] = jnp.zeros((terms_ref.shape[0] - used, LANES), jnp.float32)
-    terms_ref[used : used + RANK, :RANK] = gram
+    used = back.shape[1] // LANES
+    for block in range(used):
+        terms_ref[block] = back[:, block * LANES : (block + 1) * LANES]
+    terms_ref[used] = jnp.zeros((RANK, LANES), jnp.float32)
+    terms_ref[used, :, :RANK] = gram
 
 
 def inverse_kernel(replicas, parts_ref, out_ref):
     terms = jnp.sum(parts_ref[...], axis=0)
-    out_ref[:FEWER, :] = terms[:FEWER]
-    columns = inverse_columns(terms[FEWER : FEWER + RANK] * (1.0 / replicas))
-    for j, column in enumerate(columns):
-        out_ref[FEWER + j * RANK : FEWER + (j + 1) * RANK, :] = column
+    out_ref[:FEWER] = terms[:FEWER]
+    for j, column in enumerate(inverse_columns(terms[FEWER] * (1.0 / replicas))):
+        out_ref[FEWER + j] = column
 
 
 def error_kernel(
     replicas, terms_ref, left_ref, grads_ref, errors_ref, out_hbm, right_hbm, q_hbm, out_ref, right_ref, q_ref, sems
 ):
     rows, cols = grads_ref.shape
-    inverse = [terms_ref[SOLVER, start : start + RANK, :] for start in range(FEWER, FEWER + RANK * RANK, RANK)]
-    more = rows // LANES * RANK - FEWER
-    blocks = [terms_ref[SENDER, start : start + RANK, :] for start in range(0, more, RANK)]
-    blocks += [terms_ref[SOLVER, start : start + RANK, :] for start in range(0, FEWER, RANK)]
+    inverse = [terms_ref[SOLVER, FEWER + j] for j in range(RANK)]
+    blocks = [terms_ref[SENDER, block] for block in range(rows // LANES - FEWER)]
+    blocks += [terms_ref[SOLVER, block] for block in range(FEWER)]
     right = jnp.concatenate(
         [multiplied(inverse, left_ref[:, start : start + LANES]) for start in range(0, cols, LANES)], axis=1
     )
@@ -189,7 +188,7 @@
     replicas = lax.axis_size("z") * lax.axis_size("x")
     _, rows, cols = grads.shape
     f32, bf16 = jnp.float32, jnp.bfloat16
-    left_rows, back_rows = RANK * cols // LANES, RANK * rows // LANES
+    left_rows, back_blocks = RANK * cols // LANES, rows // LANES
     limit = pltpu.CompilerParams(vmem_limit_bytes=32 * 2**20)
     q_in, core = lax.optimization_barrier((q_in, lax.axis_index("core")))
 
@@ -212,7 +211,7 @@
         functools.partial(back_kernel, replicas),
         out_shape=(
             pltpu.VMEM((RANK, cols), f32),
-            pltpu.VMEM((back_rows + 8, LANES), f32),
+            pltpu.VMEM((back_blocks + 1, RANK, LANES), f32),
         ),
         in_specs=[VMEM] * 3,
         out_specs=(VMEM, VMEM),
@@ -225,14 +224,14 @@
     near, far = ("x", "y_low"), ("z", "y_high")
 
     def most(terms):
-        back = jnp.sum(exchange(terms[: back_rows - FEWER], near), axis=0)
+        back = jnp.sum(exchange(terms[: back_blocks - FEWER], near), axis=0)
         return jnp.sum(exchange(back, far), axis=0)
 
     def rest_and_inverse(terms):
-        terms = jnp.sum(exchange(terms[back_rows - FEWER :], far), axis=0)
+        terms = jnp.sum(exchange(terms[back_blocks - FEWER :], far), axis=0)
         return pl.pallas_call(
             functools.partial(inverse_kernel, replicas),
-            out_shape=pltpu.VMEM((FEWER + RANK * RANK, LANES), f32),
+            out_shape=pltpu.VMEM((FEWER + RANK, RANK, LANES), f32),
             in_specs=[VMEM],
             out_specs=VMEM,
             compiler_params=limit,

time: 82.7 us -> 82.5 us (level)
  no operation moved by 1% of the time
where the time goes in v4:
time: 82.5 us; the launch traced here: 82.2 us
  blocking collectives  77.6 us (94%)
  Pallas kernels  3.71 us (4%)
    all_to_all x4, blocking collectives, exchange(): return lax.all_to_all(copies, axes, 0, 0, tiled=True)  70.7 us
    all_gather x1, blocking collectives, on_device(): terms = jnp.sum(lax.all_gather(terms, 'core'), axis=0)  5.03 us
    all_gather x1, blocking collectives, on_device(): terms = lax.all_gather(terms, 'core')  1.82 us
    pallas_call x1, Pallas kernels, on_device(): pl.pallas_call(left_kernel, out_shape=(pltpu.VMEM((left_rows, LANES), f32...  1.76 us

profile of v4, /device:TPU:1, one launch (start us, length us, event | category | flops | bytes accessed | tf_op | source)
XLA Modules:
  0.0 82.2 jit_solution(2804177130509232214)
XLA Ops:
  0.6 1.8 %left.1 = (f32[16,128]{1,0:T(8,128)S(1)}, bf16[1024,512]{1,0:T(8,128)(2,1)S(1)}, bf16[1024,512]{1,0:T(8,128)(2,1)S(1)}) custom-call(f32[4,1024]{1,0:T(4,128)} %bitcast.7, bf16[1,1024,512]{2,1,0:T(8,128)(2,1)} %grads_hbm.1, bf16[1,1024,512]{2,1,0:T(8,128)(2,1)} %errors_hbm.1), custom_call_target="tpu_custom_call" | custom-call | tf_op jit(solution)/shard_map/left/pallas_call | solution.py:195
  2.4 14.3 %all_to_all.30 = f32[8,16,128]{2,1,0:T(8,128)S(1)} all-to-all(f32[8,16,128]{2,1,0:T(8,128)S(1)} %broadcast_in_dim.12), channel_id=1, replica_groups=mesh['z'=8,'x'=8,'y_high'=4,'y_low'=2,'core'=2] {'x'}, dimensions={0} | all-to-all | bytes 131072 | tf_op jit(solution)/shard_map/all_to_all | solution.py:184
  16.8 23.4 %all_to_all.31.parts_ref = f32[8,16,128]{2,1,0:T(8,128)S(1)} all-to-all(f32[8,16,128]{2,1,0:T(8,128)S(1)} %broadcast_in_dim.13), channel_id=1, replica_groups=mesh['z'=8,'x'=8,'y_high'=4,'y_low'=2,'core'=2] {'z'}, dimensions={0} | all-to-all | bytes 131072 | tf_op jit(solution)/shard_map/all_to_all | solution.py:184
  40.2 0.7 back.1
  40.9 5.0 %all-gather = f32[18,4,128]{2,1,0:T(4,128)S(1)} all-gather(f32[9,4,128]{2,1,0:T(4,128)S(1)} %get-tuple-element.24), channel_id=2, replica_groups=mesh['z'=8,'x'=8,'y_high'=4,'y_low'=2,'core'=2] {'core'}, dimensions={0}, use_global_device_ids=true | all-gather | bytes 55296 | tf_op jit(solution)/shard_map/all_gather | solution.py:222
  45.9 33.2 %conditional.1 = (f32[6,4,128]{2,1,0:T(4,128)S(1)}) conditional(s32[]{:T(128)} %convert_element_type.3, f32[9,4,128]{2,1,0:T(4,128)S(1)} %reduce_sum.46, f32[9,4,128]{2,1,0:T(4,128)S(1)} %reduce_sum.46), branch_computations={%region_2.0_spmd, %region_4.0_spmd} | conditional | flops 141312 | bytes 2433040 | solution.py:242
  46.0 11.6 %all_to_all.28 = f32[16,6,4,128]{3,2,1,0:T(4,128)S(1)} all-to-all(f32[16,6,4,128]{3,2,1,0:T(4,128)S(1)} %broadcast_in_dim.2), channel_id=1, replica_groups=mesh['z'=8,'x'=8,'y_high'=4,'y_low'=2,'core'=2] {'x','y_low'}, dimensions={0} | all-to-all | bytes 393216 | tf_op jit(solution)/shard_map/cond/branch_1_fun/all_to_all | solution.py:184
  57.7 0.1 broadcast_in_dim.3
  57.7 21.3 %all_to_all.29 = f32[32,6,4,128]{3,2,1,0:T(4,128)S(1)} all-to-all(f32[32,6,4,128]{3,2,1,0:T(4,128)S(1)} %broadcast_in_dim.3), channel_id=1, replica_groups=mesh['z'=8,'x'=8,'y_high'=4,'y_low'=2,'core'=2] {'z','y_high'}, dimensions={0} | all-to-all | bytes 786432 | tf_op jit(solution)/shard_map/cond/branch_1_fun/all_to_all | solution.py:184
  79.1 0.1 reduce_sum.42
  79.1 1.8 %all-gather.1 = f32[12,4,128]{2,1,0:T(4,128)S(1)} all-gather(f32[6,4,128]{2,1,0:T(4,128)S(1)} %get-tuple-element.32), channel_id=3, replica_groups=mesh['z'=8,'x'=8,'y_high'=4,'y_low'=2,'core'=2] {'core'}, dimensions={0}, use_global_device_ids=true | all-gather | bytes 36864 | tf_op jit(solution)/shard_map/all_gather | solution.py:243
  81.0 1.3 %error.1 = (bf16[1,1024,512]{2,1,0:T(8,128)(2,1)}, f32[4,512]{1,0:T(4,128)}, f32[4,1024]{1,0:T(4,128)}) custom-call(f32[2,6,4,128]{3,2,1,0:T(4,128)S(1)} %bitcast.5, f32[4,512]{1,0:T(4,128)S(1)} %get-tuple-element.28.left_ref, bf16[1024,512]{1,0:T(8,128)(2,1)S(1)} %get-tuple-element.22.grads_ref, bf16[1024,512]{1,0:T(8,128)(2,1)S(1)} %get-tuple-element.23.errors_ref), custom_call_target="tpu_custom_call" | custom-call | tf_op jit(solution)/shard_map/error/pallas_call | solution.py:245
  (7 shorter events, 0.1 us)
